TPU v7x, 32 devices: a whole 2x2x4 slice. The times are simulated.
32 devices in a mesh: wide: 8 (over y, x, core), narrow: 4 (over z).
Axes of the slice: x: 2, y: 2, z: 4, core: 2. Of those that a mesh axis runs over, the one named last changes fastest.
Arguments:
- velocity: bfloat16 [3, 12288, 12288], P(None, 'narrow', 'wide'), may hold values from -6 to 6
Outputs:
- dudx: bfloat16 [3, 12288, 12288], P(None, 'narrow', 'wide')
- dudy: bfloat16 [3, 12288, 12288], P(None, 'narrow', 'wide')
All inputs are finite; a program needn't handle non-finite values.
Results may differ from a plain program's by a relative error of at most 0.001.
Values may be sent and summed in bfloat16 or wider, within the bound.
A program may use at most 576 MiB of HBM per device.

v0:
```python
import math

import jax
import jax.numpy as jnp
import numpy as np
from jax import lax
from jax.experimental import pallas as pl
from jax.experimental.pallas import tpu as pltpu
from jax.sharding import PartitionSpec as P

RATIO = (math.sqrt(5.0) - 3.0) / 2.0
FACTOR = 3.0 / math.sqrt(5.0)
COEF_NEAR = 7.0 / 9.0
COEF_FAR = 1.0 / 36.0
HALO = 32
SCALE = 1.596
NUDGE = 2.0**-15
WINDOW = 256
OUT_ROWS = WINDOW - 2 * HALO
LANES = 128


def solve_weight(offset):
    return FACTOR * np.power(RATIO, np.abs(offset))


def weight_table(outputs, inputs):
    offset = np.asarray(inputs)[None, :] - np.asarray(outputs)[:, None]
    coeff = COEF_NEAR * (solve_weight(offset - 1) - solve_weight(offset + 1))
    coeff = coeff + COEF_FAR * (solve_weight(offset - 2) - solve_weight(offset + 2))
    coeff = coeff / SCALE + np.where(np.abs(offset) == 6, np.sign(offset) * NUDGE, 0.0)
    return jnp.asarray(coeff.astype(np.float32)).astype(jnp.bfloat16)


def mix(a, b):
    return lax.dot_general(a, b, (((1,), (0,)), ((), ())), preferred_element_type=jnp.float32)


def main_kernel(x_ref, prev_ref, next_ref, tx_ref, ty_ref, dx_ref, dy_ref):
    rows, cols = x_ref.shape
    for top in range(0, rows, OUT_ROWS):
        low, high = top - HALO, top - HALO + WINDOW
        parts = []
        if low < 0:
            parts.append(prev_ref[...])
        parts.append(x_ref[max(low, 0) : min(high, rows), :])
        if high > rows:
            parts.append(next_ref[...])
        window = jnp.concatenate(parts, axis=0) if len(parts) > 1 else parts[0]
        result = mix(tx_ref[...], window) * SCALE
        dx_ref[top : top + OUT_ROWS, :] = result.astype(dx_ref.dtype)
    for left in range(0, cols, 2 * LANES):
        right = min(left + 2 * LANES, cols)
        low, high = max(left - LANES, 0), min(right + LANES, cols)
        start = low - (left - LANES)
        table = ty_ref[start : start + high - low, : right - left]
        result = mix(x_ref[:, low:high], table) * SCALE
        dy_ref[:, left:right] = result.astype(dy_ref.dtype)


def edge_kernel(
    dx_in, dy_in, halo_y_ref, cur_ref, inner_ref, halo_x_ref, near_ref, far_ref,
    ty_halo_ref, ty_cur_ref, ty_in_ref, tx_halo_ref, tx_near_ref, tx_far_ref, dx_ref, dy_ref,
):
    result = lax.dot_general(
        halo_y_ref[...], ty_halo_ref[...], (((0,), (0,)), ((), ())), preferred_element_type=jnp.float32
    )
    result = result + mix(cur_ref[...], ty_cur_ref[...]) + mix(inner_ref[...], ty_in_ref[...])
    dy_ref[...] = (result * SCALE).astype(dy_ref.dtype)
    result = mix(tx_halo_ref[...], halo_x_ref[...])
    result = result + mix(tx_near_ref[...], near_ref[...]) + mix(tx_far_ref[...], far_ref[...])
    dx_ref[...] = (result * SCALE).astype(dx_ref.dtype)


def halos(ends, axis):
    devices = lax.axis_size(axis)
    up = [(i, (i + 1) % devices) for i in range(devices)]
    down = [(j, i) for i, j in up]
    leading, last = ends
    return jnp.stack([lax.ppermute(last, axis, up), lax.ppermute(leading, axis, down)])


def pick_rows(rows, limit):
    best = OUT_ROWS
    for n in range(OUT_ROWS, limit + 1, OUT_ROWS):
        if rows % n == 0:
            best = n
    return best


def shards(velocity):
    planes, rows, cols = velocity.shape
    ends_y = (
        jnp.transpose(velocity[:, :, :HALO], (0, 2, 1)),
        jnp.transpose(velocity[:, :, cols - HALO :], (0, 2, 1)),
    )
    halo_y = halos(ends_y, "wide")
    halo_x = halos((velocity[:, :HALO], velocity[:, rows - HALO :]), "narrow")

    tile = pick_rows(rows, 384)
    per = tile // HALO
    strips = rows // HALO
    tx = weight_table(np.arange(OUT_ROWS) + HALO, np.arange(WINDOW))
    ty = weight_table(np.arange(2 * LANES) + LANES, np.arange(4 * LANES)).T
    shape = jax.ShapeDtypeStruct(velocity.shape, velocity.dtype)
    full = pl.BlockSpec((None, tile, cols), lambda z, i: (z, i, 0))
    size = planes * rows * cols
    dx, dy = pl.pallas_call(
        main_kernel,
        grid=(planes, rows // tile),
        in_specs=[
            full,
            pl.BlockSpec((None, HALO, cols), lambda z, i: (z, jnp.maximum(i * per - 1, 0), 0)),
            pl.BlockSpec((None, HALO, cols), lambda z, i: (z, jnp.minimum((i + 1) * per, strips - 1), 0)),
            pl.BlockSpec(tx.shape, lambda z, i: (0, 0)),
            pl.BlockSpec(ty.shape, lambda z, i: (0, 0)),
        ],
        out_specs=[full, full],
        out_shape=[shape, shape],
        cost_estimate=pl.CostEstimate(flops=size * 2 * 1024, bytes_accessed=size * 6, transcendentals=0),
        compiler_params=pltpu.CompilerParams(vmem_limit_bytes=48 * 2**20),
    )(velocity, velocity, velocity, tx, ty)

    here = np.arange(LANES)
    before, after = (np.arange(-HALO, 0), np.arange(LANES, LANES + HALO))
    ty_halo = jnp.stack([weight_table(here, before).T, weight_table(here, after).T])
    ty_cur = weight_table(here, here).T
    ty_in = jnp.stack([weight_table(here, here + LANES).T, weight_table(here, here - LANES).T])
    edge = np.arange(HALO)
    tx_halo = jnp.stack([weight_table(edge, edge - HALO), weight_table(edge, edge + HALO)])
    tx_near = weight_table(edge, edge)
    tx_far = jnp.stack([weight_table(edge, edge + HALO), weight_table(edge, edge - HALO)])
    blocks = cols // LANES

    def whole(table):
        return pl.BlockSpec(table.shape, lambda s, z: (0, 0))

    def sided(table):
        return pl.BlockSpec((None,) + table.shape[1:], lambda s, z: (s, 0, 0))

    lanes_out = pl.BlockSpec((None, rows, LANES), lambda s, z: (z, 0, s * (blocks - 1)))
    rows_out = pl.BlockSpec((None, HALO, cols), lambda s, z: (z, s * (strips - 1), 0))
    any_spec = pl.BlockSpec(memory_space=pl.ANY)
    return pl.pallas_call(
        edge_kernel,
        grid=(2, planes),
        in_specs=[
            any_spec,
            any_spec,
            pl.BlockSpec((None, None, HALO, rows), lambda s, z: (s, z, 0, 0)),
            lanes_out,
            pl.BlockSpec((None, rows, LANES), lambda s, z: (z, 0, s * (blocks - 3) + 1)),
            pl.BlockSpec((None, None, HALO, cols), lambda s, z: (s, z, 0, 0)),
            rows_out,
            pl.BlockSpec((None, HALO, cols), lambda s, z: (z, s * (strips - 3) + 1, 0)),
            sided(ty_halo), whole(ty_cur), sided(ty_in), sided(tx_halo), whole(tx_near), sided(tx_far),
        ],
        out_specs=[rows_out, lanes_out],
        out_shape=[shape, shape],
        input_output_aliases={0: 0, 1: 1},
        cost_estimate=pl.CostEstimate(flops=size * 64, bytes_accessed=size, transcendentals=0),
        compiler_params=pltpu.CompilerParams(vmem_limit_bytes=48 * 2**20),
    )(dx, dy, halo_y, velocity, velocity, halo_x, velocity, velocity,
      ty_halo, ty_cur, ty_in, tx_halo, tx_near, tx_far)


def solution(mesh):
    placed = P(None, "narrow", "wide")
    return jax.shard_map(
        shards, mesh=mesh, in_specs=(placed,), out_specs=(placed, placed), check_vma=False
    )
```

profile of v0, /device:TPU:0, one launch (start us, length us, event | category | flops | bytes accessed | tf_op | source)
XLA Modules:
  0.0 72.2 jit_solution(6423596067933720282)
XLA Ops:
  0.6 1.9 %fusion = (bf16[3,32,1536]{2,1,0:T(8,128)(2,1)}, bf16[3,32,1536]{2,1,0:T(8,128)(2,1)}) fusion(bf16[3,3072,1536]{2,1,0:T(8,128)(2,1)} %far_ref.1), kind=kLoop, calls=%fused_computation.2 | loop fusion | bytes 1179648 | tf_op jit(solution)/shard_map/slice | solution.py:98
  2.6 3.0 %collective-permute-start.2 = (bf16[3,32,1536]{2,1,0:T(8,128)(2,1)}, bf16[3,32,1536]{2,1,0:T(8,128)(2,1)}, u32[]{:S(2)}, u32[]{:S(2)}) collective-permute-start(bf16[3,32,1536]{2,1,0:T(8,128)(2,1)} %get-tuple-element.6), channel_id=1, source_target_pairs={{0,1},{1,2},{2,3},{3,0},{4,5},{5,6},{6,7},{7,4},{8,9},{9,10},{10,1... | collective-permute-start | bytes 884744 | tf_op jit(solution)/shard_map/ppermute | solution.py:80
  5.6 2.0 %collective-permute-start.3 = (bf16[3,32,1536]{2,1,0:T(8,128)(2,1)}, bf16[3,32,1536]{2,1,0:T(8,128)(2,1)}, u32[]{:S(2)}, u32[]{:S(2)}) collective-permute-start(bf16[3,32,1536]{2,1,0:T(8,128)(2,1)} %get-tuple-element.7), channel_id=1, source_target_pairs={{1,0},{2,1},{3,2},{0,3},{5,4},{6,5},{7,6},{4,7},{9,8},{10,9},{11,1... | collective-permute-start | bytes 884744 | tf_op jit(solution)/shard_map/ppermute | solution.py:80
  7.6 4.6 %fusion.1 = (bf16[3,3072,32]{2,1,0:T(8,128)(2,1)S(1)}, bf16[3,3072,32]{2,1,0:T(8,128)(2,1)}) fusion(bf16[3,3072,1536]{2,1,0:T(8,128)(2,1)} %far_ref.1), kind=kLoop, calls=%fused_computation.3 | loop fusion | bytes 2359296 | tf_op jit(solution)/shard_map/slice | solution.py:95
  12.2 0.0 copy-start.6
  12.2 0.0 copy-start.7
  12.2 2.8 %copy.20 = bf16[3,3072,32]{1,2,0:T(8,128)(2,1)} copy(bf16[3,3072,32]{2,1,0:T(8,128)(2,1)} %get-tuple-element.9) | data formatting | bytes 1179648
  15.0 1.6 %collective-permute-start.1 = (bf16[3,32,3072]{2,1,0:T(8,128)(2,1)}, bf16[3,32,3072]{2,1,0:T(8,128)(2,1)S(1)}, u32[]{:S(2)}, u32[]{:S(2)}) collective-permute-start(bf16[3,32,3072]{2,1,0:T(8,128)(2,1)} %bitcast.7), channel_id=1, source_target_pairs={{4,0},{8,4},{12,8},{16,12},{20,16},{24,20},{28,24},{0,28},{5,1},{9... | collective-permute-start | bytes 1769480 | tf_op jit(solution)/shard_map/ppermute | solution.py:80
  16.6 1.6 %copy.19 = bf16[3,3072,32]{1,2,0:T(8,128)(2,1)} copy(bf16[3,3072,32]{2,1,0:T(8,128)(2,1)S(1)} %get-tuple-element.8) | data formatting | bytes 1179648
  18.2 0.0 collective-permute-start
  18.2 0.0 copy-done.6
  18.2 0.0 copy-done.7
  18.3 42.8 %shard_map.140 = (bf16[3,3072,1536]{2,1,0:T(8,128)(2,1)}, bf16[3,3072,1536]{2,1,0:T(8,128)(2,1)}) custom-call(bf16[3,3072,1536]{2,1,0:T(8,128)(2,1)} %far_ref.1, bf16[3,3072,1536]{2,1,0:T(8,128)(2,1)} %far_ref.1, bf16[3,3072,1536]{2,1,0:T(8,128)(2,1)} %far_ref.1, bf16[192,256]{1,0:T(8,128)(2,1)S(1)} %copy-done.7, bf16[512,256]{1,0:T(8,128)(2,1)S(1)} %copy-done.6), custom_call_target="tpu_custom_call" | custom-call | flops 28991029248 | bytes 84934656 | tf_op jit(solution)/shard_map/pallas_call | solution.py:108
  61.0 0.0 copy-start
  61.0 0.0 copy-start.1
  61.0 0.0 copy-start.2
  61.0 0.0 copy-start.3
  61.1 0.0 copy-start.4
  61.1 0.0 copy-start.5
  61.1 0.0 collective-permute-done.2
  61.1 0.0 collective-permute-done.3
  61.1 1.1 %pad_maximum_fusion.1.halo_x_ref = bf16[2,3,32,1536]{3,2,1,0:T(8,128)(2,1)S(1)} fusion(bf16[1,3,32,1536]{3,2,1,0:T(8,128)(2,1)} %bitcast.5, bf16[1,3,32,1536]{3,2,1,0:T(8,128)(2,1)} %bitcast.4), kind=kLoop, calls=%fused_computation.1 | loop fusion | flops 294912 | bytes 1179648 | tf_op jit(solution)/shard_map/stack | solution.py:80
  62.3 0.0 collective-permute-done.1
  62.3 0.0 collective-permute-done
  62.3 0.1 pad_maximum_fusion.halo_y_ref
  62.4 0.0 copy-done
  62.4 0.0 copy-done.1
  62.4 0.0 copy-done.2
  62.4 0.0 copy-done.3
  62.4 0.0 copy-done.4
  62.4 0.0 copy-done.5
  62.5 9.7 %shard_map.141 = (bf16[3,3072,1536]{2,1,0:T(8,128)(2,1)}, bf16[3,3072,1536]{2,1,0:T(8,128)(2,1)}) custom-call(bf16[3,3072,1536]{2,1,0:T(8,128)(2,1)} %get-tuple-element.4.dx_in, bf16[3,3072,1536]{2,1,0:T(8,128)(2,1)} %get-tuple-element.5.dy_in, ...), custom_call_target="tpu_custom_call", output_to_operand_aliasing={{0}: (0, {}), {1}: (1, {})} | custom-call | flops 905969664 | bytes 14155776 | tf_op jit(solution)/shard_map/pallas_call | solution.py:144
Async XLA Ops:
  2.6 58.5 %collective-permute-start.2 = (bf16[3,32,1536]{2,1,0:T(8,128)(2,1)}, bf16[3,32,1536]{2,1,0:T(8,128)(2,1)}, u32[]{:S(2)}, u32[]{:S(2)}) collective-permute-start(bf16[3,32,1536]{2,1,0:T(8,128)(2,1)} %get-tuple-element.6), channel_id=1, source_target_pairs={{0,1},{1,2},{2,3},{3,0},{4,5},{5,6},{6,7},{7,4},{8,9},{9,10},{10,1... | collective-permute-start | bytes 884744 | tf_op jit(solution)/shard_map/ppermute | solution.py:80
  5.6 55.5 %collective-permute-start.3 = (bf16[3,32,1536]{2,1,0:T(8,128)(2,1)}, bf16[3,32,1536]{2,1,0:T(8,128)(2,1)}, u32[]{:S(2)}, u32[]{:S(2)}) collective-permute-start(bf16[3,32,1536]{2,1,0:T(8,128)(2,1)} %get-tuple-element.7), channel_id=1, source_target_pairs={{1,0},{2,1},{3,2},{0,3},{5,4},{6,5},{7,6},{4,7},{9,8},{10,9},{11,1... | collective-permute-start | bytes 884744 | tf_op jit(solution)/shard_map/ppermute | solution.py:80
  12.2 6.0 %copy-start.6 = (bf16[512,256]{1,0:T(8,128)(2,1)S(1)}, bf16[512,256]{1,0:T(8,128)(2,1)}, u32[]{:S(2)}) copy-start(bf16[512,256]{1,0:T(8,128)(2,1)} %constant.32.ty_ref) | copy-start | bytes 786436
  12.2 6.0 %copy-start.7 = (bf16[192,256]{1,0:T(8,128)(2,1)S(1)}, bf16[192,256]{1,0:T(8,128)(2,1)}, u32[]{:S(2)}) copy-start(bf16[192,256]{1,0:T(8,128)(2,1)} %constant.30.tx_ref) | copy-start | bytes 294916
  15.0 47.2 %collective-permute-start.1 = (bf16[3,32,3072]{2,1,0:T(8,128)(2,1)}, bf16[3,32,3072]{2,1,0:T(8,128)(2,1)S(1)}, u32[]{:S(2)}, u32[]{:S(2)}) collective-permute-start(bf16[3,32,3072]{2,1,0:T(8,128)(2,1)} %bitcast.7), channel_id=1, source_target_pairs={{4,0},{8,4},{12,8},{16,12},{20,16},{24,20},{28,24},{0,28},{5,1},{9... | collective-permute-start | bytes 1769480 | tf_op jit(solution)/shard_map/ppermute | solution.py:80
  18.2 44.0 %collective-permute-start = (bf16[3,32,3072]{2,1,0:T(8,128)(2,1)}, bf16[3,32,3072]{2,1,0:T(8,128)(2,1)S(1)}, u32[]{:S(2)}, u32[]{:S(2)}) collective-permute-start(bf16[3,32,3072]{2,1,0:T(8,128)(2,1)} %bitcast.9), channel_id=1, source_target_pairs={{0,4},{4,8},{8,12},{12,16},{16,20},{20,24},{24,28},{28,0},{1,5},{5... | collective-permute-start | bytes 1769480 | tf_op jit(solution)/shard_map/ppermute | solution.py:80
  61.0 1.4 %copy-start = (bf16[2,128,128]{2,1,0:T(8,128)(2,1)S(1)}, bf16[2,128,128]{2,1,0:T(8,128)(2,1)}, u32[]{:S(2)}) copy-start(bf16[2,128,128]{2,1,0:T(8,128)(2,1)} %constant.48.ty_in_ref) | copy-start | bytes 196612
  61.0 1.4 %copy-start.1 = (bf16[128,128]{1,0:T(8,128)(2,1)S(1)}, bf16[128,128]{1,0:T(8,128)(2,1)}, u32[]{:S(2)}) copy-start(bf16[128,128]{1,0:T(8,128)(2,1)} %constant.41.ty_cur_ref) | copy-start | bytes 98308
  61.0 1.4 %copy-start.2 = (bf16[2,32,32]{2,1,0:T(8,128)(2,1)S(1)}, bf16[2,32,32]{2,1,0:T(8,128)(2,1)}, u32[]{:S(2)}) copy-start(bf16[2,32,32]{2,1,0:T(8,128)(2,1)} %constant.55.tx_far_ref) | copy-start | bytes 12292
  61.0 1.4 %copy-start.3 = (bf16[2,32,32]{2,1,0:T(8,128)(2,1)S(1)}, bf16[2,32,32]{2,1,0:T(8,128)(2,1)}, u32[]{:S(2)}) copy-start(bf16[2,32,32]{2,1,0:T(8,128)(2,1)} %constant.53.tx_halo_ref) | copy-start | bytes 12292
  61.1 1.4 %copy-start.4 = (bf16[2,32,128]{2,1,0:T(8,128)(2,1)S(1)}, bf16[2,32,128]{2,1,0:T(8,128)(2,1)}, u32[]{:S(2)}) copy-start(bf16[2,32,128]{2,1,0:T(8,128)(2,1)} %constant.39.ty_halo_ref) | copy-start | bytes 49156
  61.1 1.4 %copy-start.5 = (bf16[32,32]{1,0:T(8,128)(2,1)S(1)}, bf16[32,32]{1,0:T(8,128)(2,1)}, u32[]{:S(2)}) copy-start(bf16[32,32]{1,0:T(8,128)(2,1)} %constant.54.tx_near_ref) | copy-start | bytes 6148
where the time goes:
time: 73.1 us; the launch traced here: 72.2 us
  Pallas kernels  52.5 us (72%)
  local copies, waits for them, and re-layouts  11 us (15%)
  starting transfers between devices  6.66 us (9%)
  other arithmetic  1.26 us (2%)
  between operations  0.76 us (1%)
    pallas_call x1, Pallas kernels, shards(): pl.pallas_call(main_kernel, grid=(planes, rows // tile), in_specs=[full,...  42.8 us
    pallas_call x1, Pallas kernels, shards(): pl.pallas_call(edge_kernel, grid=(2, planes), in_specs=[any_spec, any_spe...  9.73 us
    slice x1, local copies, waits for them, and re-layouts, shards(): velocity[:, :, cols - HALO:]  4.61 us
    unnamed x18, local copies, waits for them, and re-layouts  4.43 us
    ppermute x2, starting transfers between devices, halos(): lax.ppermute(leading, axis, down)  3.63 us
    ppermute x2, starting transfers between devices, halos(): lax.ppermute(last, axis, up)  3.03 us
    slice x1, local copies, waits for them, and re-layouts, shards(): halo_x = halos((velocity[:, :HALO], velocity[:, rows - HALO:]), 'narrow')  1.94 us
  transfers between devices with their start and end apart: 4, of which 0 were waited for; matrix products, arithmetic and copies ran while one was open for 14% of the time, Pallas kernels for 59%

commit v1 on v0

v1 whole, which is shorter than its diff:
```python
import math

import jax
import jax.numpy as jnp
import numpy as np
from jax import lax
from jax.experimental import pallas as pl
from jax.experimental.pallas import tpu as pltpu
from jax.sharding import PartitionSpec as P

RATIO = (math.sqrt(5.0) - 3.0) / 2.0
FACTOR = 3.0 / math.sqrt(5.0)
COEF_NEAR = 7.0 / 9.0
COEF_FAR = 1.0 / 36.0
HALO = 32
SCALE = 1.596
NUDGE = 2.0**-15
WINDOW = 256
PACK = 16
OUT_ROWS = WINDOW - 2 * HALO
LANES = 128


def solve_weight(offset):
    return FACTOR * np.power(RATIO, np.abs(offset))


def weight_table(outputs, inputs):
    offset = np.asarray(inputs)[None, :] - np.asarray(outputs)[:, None]
    coeff = COEF_NEAR * (solve_weight(offset - 1) - solve_weight(offset + 1))
    coeff = coeff + COEF_FAR * (solve_weight(offset - 2) - solve_weight(offset + 2))
    coeff = coeff / SCALE + np.where(np.abs(offset) == 6, np.sign(offset) * NUDGE, 0.0)
    return jnp.asarray(coeff.astype(np.float32)).astype(jnp.bfloat16)


def mix(a, b):
    return lax.dot_general(a, b, (((1,), (0,)), ((), ())), preferred_element_type=jnp.float32)


def pack_tables():
    cell = np.arange(LANES)
    lead, last = (np.zeros((PACK, LANES)), np.zeros((PACK, LANES)))
    for i in range(PACK - 1):
        lead[i, i] = 1.0
        last[PACK - 1 - i, LANES - 1 - i] = 1.0
    tail = np.where(cell >= PACK - 1, np.power(RATIO, np.maximum(cell - PACK + 1, 0)), 0.0)
    lead[PACK - 1], last[0] = (tail, tail[::-1])
    return jnp.asarray(np.stack([last, lead]).astype(np.float32)).astype(jnp.bfloat16)


def exchange_kernel(
    x_ref, table_ref, halo_y_ref, halo_x_ref,
    edge_y, edge_x, out_y, out_x, load_sem, send_sem, recv_sem,
):
    planes, rows, cols = x_ref.shape
    depth = edge_x.shape[2]
    loads = []
    for z in range(planes):
        for side in range(2):
            col = (cols - LANES) if side == 0 else 0
            row = (rows - depth) if side == 0 else 0
            loads.append(pltpu.make_async_copy(
                x_ref.at[z, :, pl.ds(col, LANES)], edge_y.at[side, z], load_sem.at[0, side, z]))
            loads.append(pltpu.make_async_copy(
                x_ref.at[z, pl.ds(row, depth), :], edge_x.at[side, z], load_sem.at[1, side, z]))
    for load in loads:
        load.start()

    targets = []
    for axis in ("wide", "narrow"):
        size = lax.axis_size(axis)
        me = lax.axis_index(axis)
        targets.append(({axis: lax.rem(me + 1, size)}, {axis: lax.rem(me + size - 1, size)}))
    barrier = pltpu.get_barrier_semaphore()
    for pair in targets:
        for target in pair:
            pl.semaphore_signal(barrier, inc=1, device_id=target, device_id_type=pl.DeviceIdType.MESH)
    pl.semaphore_wait(barrier, 4)

    sends = []
    at = 0
    for z in range(planes):
        for side in range(2):
            loads[at].wait()
            packed = lax.dot_general(
                table_ref[side], edge_y[side, z], (((1,), (1,)), ((), ())),
                preferred_element_type=jnp.float32)
            out_y[side, z] = packed.astype(out_y.dtype)
            sends.append(pltpu.make_async_remote_copy(
                out_y.at[side, z], halo_y_ref.at[side, z], send_sem.at[0, side, z],
                recv_sem.at[0, side, z], device_id=targets[0][side],
                device_id_type=pl.DeviceIdType.MESH))
            sends[-1].start()
            loads[at + 1].wait()
            cut = (LANES - depth) if side == 0 else 0
            packed = mix(table_ref[side][:, cut : cut + depth], edge_x[side, z])
            out_x[side, z] = packed.astype(out_x.dtype)
            sends.append(pltpu.make_async_remote_copy(
                out_x.at[side, z], halo_x_ref.at[side, z], send_sem.at[1, side, z],
                recv_sem.at[1, side, z], device_id=targets[1][side],
                device_id_type=pl.DeviceIdType.MESH))
            sends[-1].start()
            at += 2
    for send in sends:
        send.wait()


def exchange(velocity):
    planes, rows, cols = velocity.shape
    depth = LANES
    dtype = velocity.dtype
    shape_y, shape_x = ((2, planes, PACK, rows), (2, planes, PACK, cols))
    return pl.pallas_call(
        exchange_kernel,
        in_specs=[pl.BlockSpec(memory_space=pl.ANY), pl.BlockSpec(memory_space=pltpu.VMEM)],
        out_specs=[pl.BlockSpec(memory_space=pl.ANY)] * 2,
        out_shape=[jax.ShapeDtypeStruct(shape_y, dtype), jax.ShapeDtypeStruct(shape_x, dtype)],
        scratch_shapes=[
            pltpu.VMEM((2, planes, rows, LANES), dtype),
            pltpu.VMEM((2, planes, depth, cols), dtype),
            pltpu.VMEM(shape_y, dtype),
            pltpu.VMEM(shape_x, dtype),
            pltpu.SemaphoreType.DMA((2, 2, planes)),
            pltpu.SemaphoreType.DMA((2, 2, planes)),
            pltpu.SemaphoreType.DMA((2, 2, planes)),
        ],
        compiler_params=pltpu.CompilerParams(
            collective_id=0, has_side_effects=True, vmem_limit_bytes=48 * 2**20),
    )(velocity, pack_tables())


def main_kernel(
    x_ref, prev_ref, next_ref, before_x_ref, after_x_ref, before_y_ref, after_y_ref,
    tx_ref, ty_ref, th_ref, dx_ref, dy_ref,
):
    rows, cols = x_ref.shape
    step, steps = (pl.program_id(1), pl.num_programs(1))
    empty = jnp.zeros((HALO - PACK, cols), x_ref.dtype)
    for top in range(0, rows, OUT_ROWS):
        low, high = top - HALO, top - HALO + WINDOW
        parts = []
        if low < 0:
            outside = jnp.concatenate([empty, before_x_ref[...]], axis=0)
            parts.append(jnp.where(step == 0, outside, prev_ref[...]))
        parts.append(x_ref[max(low, 0) : min(high, rows), :])
        if high > rows:
            outside = jnp.concatenate([after_x_ref[...], empty], axis=0)
            parts.append(jnp.where(step == steps - 1, outside, next_ref[...]))
        window = jnp.concatenate(parts, axis=0) if len(parts) > 1 else parts[0]
        result = mix(tx_ref[...], window) * SCALE
        dx_ref[top : top + OUT_ROWS, :] = result.astype(dx_ref.dtype)
    for left in range(0, cols, 2 * LANES):
        right = min(left + 2 * LANES, cols)
        low, high = max(left - LANES, 0), min(right + LANES, cols)
        start = low - (left - LANES)
        table = ty_ref[start : start + high - low, : right - left]
        result = mix(x_ref[:, low:high], table)
        blocks = [result[:, k : k + LANES] for k in range(0, right - left, LANES)]
        if left == 0:
            blocks[0] = blocks[0] + mix_first(before_y_ref[...], th_ref[0])
        if right == cols:
            blocks[-1] = blocks[-1] + mix_first(after_y_ref[...], th_ref[1])
        for k, block in enumerate(blocks):
            dy_ref[:, left + k * LANES : left + (k + 1) * LANES] = (block * SCALE).astype(dy_ref.dtype)


def mix_first(a, b):
    return lax.dot_general(a, b, (((0,), (0,)), ((), ())), preferred_element_type=jnp.float32)


def pick_rows(rows, limit):
    best = OUT_ROWS
    for n in range(OUT_ROWS, limit + 1, OUT_ROWS):
        if rows % n == 0:
            best = n
    return best


def shards(velocity):
    planes, rows, cols = velocity.shape
    halo_y, halo_x = exchange(velocity)
    tile = pick_rows(rows, 768)
    per = tile // HALO
    strips = rows // HALO
    tx = weight_table(np.arange(OUT_ROWS) + HALO, np.arange(WINDOW))
    ty = weight_table(np.arange(2 * LANES) + LANES, np.arange(4 * LANES)).T
    here = np.arange(LANES)
    th = jnp.stack([
        weight_table(here, np.arange(-PACK, 0)).T,
        weight_table(here, np.arange(LANES, LANES + PACK)).T,
    ])
    shape = jax.ShapeDtypeStruct(velocity.shape, velocity.dtype)
    full = pl.BlockSpec((None, tile, cols), lambda z, i: (z, i, 0))
    size = planes * rows * cols

    def ends_x(side):
        return pl.BlockSpec((None, None, PACK, cols), lambda z, i: (side, z, 0, 0))

    def ends_y(side):
        return pl.BlockSpec((None, None, PACK, tile), lambda z, i: (side, z, 0, i))

    return pl.pallas_call(
        main_kernel,
        grid=(planes, rows // tile),
        in_specs=[
            full,
            pl.BlockSpec((None, HALO, cols), lambda z, i: (z, jnp.maximum(i * per - 1, 0), 0)),
            pl.BlockSpec((None, HALO, cols), lambda z, i: (z, jnp.minimum((i + 1) * per, strips - 1), 0)),
            ends_x(0), ends_x(1), ends_y(0), ends_y(1),
            pl.BlockSpec(tx.shape, lambda z, i: (0, 0)),
            pl.BlockSpec(ty.shape, lambda z, i: (0, 0)),
            pl.BlockSpec(th.shape, lambda z, i: (0, 0, 0)),
        ],
        out_specs=[full, full],
        out_shape=[shape, shape],
        cost_estimate=pl.CostEstimate(flops=size * 2 * 1024, bytes_accessed=size * 6, transcendentals=0),
        compiler_params=pltpu.CompilerParams(vmem_limit_bytes=48 * 2**20),
    )(velocity, velocity, velocity, halo_x, halo_x, halo_y, halo_y, tx, ty, th)


def solution(mesh):
    placed = P(None, "narrow", "wide")
    return jax.shard_map(
        shards, mesh=mesh, in_specs=(placed,), out_specs=(placed, placed), check_vma=False
    )
```

time: 73.1 us -> 53.3 us (0.73)
  local copies, waits for them, and re-layouts: 11 us -> 0.7 us
  starting transfers between devices: 6.66 us -> 0 us
  other arithmetic: 1.26 us -> 0 us
  Pallas kernels: 52.5 us -> 51.4 us
    ppermute x4 -> x0, starting transfers between devices: 6.66 us -> none  [the longest x2 3.63 us: halos(): lax.ppermute(leading, axis, down)]
    slice x2 -> x0, local copies, waits for them, and re-layouts: 6.55 us -> none  [the longest x1 4.61 us: shards(): velocity[:, :, cols - HALO:]]
    pallas_call x1, Pallas kernels: 42.8 us -> 37.3 us  [shards(): pl.pallas_call(main_kernel, grid=(planes, rows // tile), in_specs=[full,...]
    pallas_call x1, Pallas kernels: 9.73 us -> 14.1 us  [exchange(): pl.pallas_call(exchange_kernel, in_specs=[pl.BlockSpec(memory_space=pl.AN...]
    unnamed x18 -> x8, local copies, waits for them, and re-layouts: 4.43 us -> 0.7 us
    another operation x2 -> x0, other arithmetic: 1.26 us -> none  [halos(): jnp.stack([lax.ppermute(last, axis, up), lax.ppermute(leading, axis, down)])]
  transfers between devices with their start and end apart: 4 -> 0, of which waited for: 0 -> 0; matrix products, arithmetic and copies ran while one was open for 14% -> 0% of each run, Pallas kernels for 59% -> 0%
where the time goes in v1:
time: 53.3 us; the launch traced here: 52.8 us
  Pallas kernels  51.4 us (96%)
  local copies, waits for them, and re-layouts  0.7 us (1%)
  between operations  0.67 us (1%)
    pallas_call x1, Pallas kernels, shards(): pl.pallas_call(main_kernel, grid=(planes, rows // tile), in_specs=[full,...  37.3 us
    pallas_call x1, Pallas kernels, exchange(): pl.pallas_call(exchange_kernel, in_specs=[pl.BlockSpec(memory_space=pl.AN...  14.1 us

profile of v1, /device:TPU:0, one launch (start us, length us, event | category | flops | bytes accessed | tf_op | source)
XLA Modules:
  0.0 52.8 jit_solution(10771964476550617272)
XLA Ops:
  0.6 0.0 copy-start
  0.6 0.7 %copy-done = bf16[2,16,128]{2,1,0:T(8,128)(2,1)S(1)} copy-done((bf16[2,16,128]{2,1,0:T(8,128)(2,1)S(1)}, bf16[2,16,128]{2,1,0:T(8,128)(2,1)}, u32[]{:S(2)}) %copy-start) | copy-done | bytes 8216
  1.3 0.0 copy-start.1
  1.3 0.0 copy-start.2
  1.3 0.0 copy-start.3
  1.3 14.1 %shard_map.77 = (bf16[2,3,16,3072]{3,2,1,0:T(8,128)(2,1)S(1)}, bf16[2,3,16,1536]{3,2,1,0:T(8,128)(2,1)S(1)}) custom-call(bf16[3,3072,1536]{2,1,0:T(8,128)(2,1)} %next_ref.1, bf16[2,16,128]{2,1,0:T(8,128)(2,1)S(1)} %copy-done), custom_call_target="tpu_custom_call" | custom-call | tf_op jit(solution)/shard_map/pallas_call | solution.py:113
  15.5 0.0 copy-done.1
  15.5 0.0 copy-done.2
  15.5 0.0 copy-done.3
  15.5 37.3 %shard_map.78 = (bf16[3,3072,1536]{2,1,0:T(8,128)(2,1)}, bf16[3,3072,1536]{2,1,0:T(8,128)(2,1)}) custom-call(bf16[3,3072,1536]{2,1,0:T(8,128)(2,1)} %next_ref.1, bf16[3,3072,1536]{2,1,0:T(8,128)(2,1)} %next_ref.1, bf16[3,3072,1536]{2,1,0:T(8,128)(2,1)} %next_ref.1, bf16[2,3,16,1536]{3,2,1,0:T(8,128)(2,1)S(1)} %get-tuple-element.4.before_x_ref.after_x_ref, ...), custom_call_target="tpu_custom_call" | custom-call | flops 28991029248 | bytes 84934656 | tf_op jit(solution)/shard_map/pallas_call | solution.py:202
Async XLA Ops:
  0.6 0.7 %copy-start = (bf16[2,16,128]{2,1,0:T(8,128)(2,1)S(1)}, bf16[2,16,128]{2,1,0:T(8,128)(2,1)}, u32[]{:S(2)}) copy-start(bf16[2,16,128]{2,1,0:T(8,128)(2,1)} %constant.15.table_ref) | copy-start | bytes 24580
  1.3 14.2 %copy-start.1 = (bf16[512,256]{1,0:T(8,128)(2,1)S(1)}, bf16[512,256]{1,0:T(8,128)(2,1)}, u32[]{:S(2)}) copy-start(bf16[512,256]{1,0:T(8,128)(2,1)} %constant.18.ty_ref) | copy-start | bytes 786436
  1.3 14.2 %copy-start.2 = (bf16[192,256]{1,0:T(8,128)(2,1)S(1)}, bf16[192,256]{1,0:T(8,128)(2,1)}, u32[]{:S(2)}) copy-start(bf16[192,256]{1,0:T(8,128)(2,1)} %constant.16.tx_ref) | copy-start | bytes 294916
  1.3 14.2 %copy-start.3 = (bf16[2,16,128]{2,1,0:T(8,128)(2,1)S(1)}, bf16[2,16,128]{2,1,0:T(8,128)(2,1)}, u32[]{:S(2)}) copy-start(bf16[2,16,128]{2,1,0:T(8,128)(2,1)} %constant.25.th_ref) | copy-start | bytes 24580

commit v2 on v1

--- a/solution.py
+++ b/solution.py
@@ -63,9 +63,6 @@
                 x_ref.at[z, :, pl.ds(col, LANES)], edge_y.at[side, z], load_sem.at[0, side, z]))
             loads.append(pltpu.make_async_copy(
                 x_ref.at[z, pl.ds(row, depth), :], edge_x.at[side, z], load_sem.at[1, side, z]))
-    for load in loads:
-        load.start()
-
     targets = []
     for axis in ("wide", "narrow"):
         size = lax.axis_size(axis)
@@ -75,8 +72,9 @@
     for pair in targets:
         for target in pair:
             pl.semaphore_signal(barrier, inc=1, device_id=target, device_id_type=pl.DeviceIdType.MESH)
-    pl.semaphore_wait(barrier, 4)
-
+
+    for load in loads:
+        load.start()
     sends = []
     at = 0
     for z in range(planes):
@@ -86,6 +84,8 @@
                 table_ref[side], edge_y[side, z], (((1,), (1,)), ((), ())),
                 preferred_element_type=jnp.float32)
             out_y[side, z] = packed.astype(out_y.dtype)
+            if not sends:
+                pl.semaphore_wait(barrier, 4)
             sends.append(pltpu.make_async_remote_copy(
                 out_y.at[side, z], halo_y_ref.at[side, z], send_sem.at[0, side, z],
                 recv_sem.at[0, side, z], device_id=targets[0][side],
@@ -107,7 +107,7 @@
 
 def exchange(velocity):
     planes, rows, cols = velocity.shape
-    depth = LANES
+    depth = LANES // 2
     dtype = velocity.dtype
     shape_y, shape_x = ((2, planes, PACK, rows), (2, planes, PACK, cols))
     return pl.pallas_call(

time: 53.3 us -> 53 us (level)
  no operation moved by 1% of the time
where the time goes in v2:
time: 53 us; the launch traced here: 52.5 us
  Pallas kernels  51.1 us (96%)
  local copies, waits for them, and re-layouts  0.7 us (1%)
  between operations  0.67 us (1%)
    pallas_call x1, Pallas kernels, shards(): pl.pallas_call(main_kernel, grid=(planes, rows // tile), in_specs=[full,...  37.3 us
    pallas_call x1, Pallas kernels, exchange(): pl.pallas_call(exchange_kernel, in_specs=[pl.BlockSpec(memory_space=pl.AN...  13.8 us

profile of v2, /device:TPU:0, one launch (start us, length us, event | category | flops | bytes accessed | tf_op | source)
XLA Modules:
  0.0 52.5 jit_solution(11313299686011572773)
XLA Ops:
  0.6 0.0 copy-start
  0.6 0.7 %copy-done = bf16[2,16,128]{2,1,0:T(8,128)(2,1)S(1)} copy-done((bf16[2,16,128]{2,1,0:T(8,128)(2,1)S(1)}, bf16[2,16,128]{2,1,0:T(8,128)(2,1)}, u32[]{:S(2)}) %copy-start) | copy-done | bytes 8216
  1.3 0.0 copy-start.1
  1.3 0.0 copy-start.2
  1.3 0.0 copy-start.3
  1.3 13.8 %shard_map.77 = (bf16[2,3,16,3072]{3,2,1,0:T(8,128)(2,1)S(1)}, bf16[2,3,16,1536]{3,2,1,0:T(8,128)(2,1)S(1)}) custom-call(bf16[3,3072,1536]{2,1,0:T(8,128)(2,1)} %next_ref.1, bf16[2,16,128]{2,1,0:T(8,128)(2,1)S(1)} %copy-done), custom_call_target="tpu_custom_call" | custom-call | tf_op jit(solution)/shard_map/pallas_call | solution.py:113
  15.2 0.0 copy-done.1
  15.2 0.0 copy-done.2
  15.2 0.0 copy-done.3
  15.2 37.3 %shard_map.78 = (bf16[3,3072,1536]{2,1,0:T(8,128)(2,1)}, bf16[3,3072,1536]{2,1,0:T(8,128)(2,1)}) custom-call(bf16[3,3072,1536]{2,1,0:T(8,128)(2,1)} %next_ref.1, bf16[3,3072,1536]{2,1,0:T(8,128)(2,1)} %next_ref.1, bf16[3,3072,1536]{2,1,0:T(8,128)(2,1)} %next_ref.1, bf16[2,3,16,1536]{3,2,1,0:T(8,128)(2,1)S(1)} %get-tuple-element.4.before_x_ref.after_x_ref, ...), custom_call_target="tpu_custom_call" | custom-call | flops 28991029248 | bytes 84934656 | tf_op jit(solution)/shard_map/pallas_call | solution.py:202
Async XLA Ops:
  0.6 0.7 %copy-start = (bf16[2,16,128]{2,1,0:T(8,128)(2,1)S(1)}, bf16[2,16,128]{2,1,0:T(8,128)(2,1)}, u32[]{:S(2)}) copy-start(bf16[2,16,128]{2,1,0:T(8,128)(2,1)} %constant.15.table_ref) | copy-start | bytes 24580
  1.3 13.8 %copy-start.1 = (bf16[512,256]{1,0:T(8,128)(2,1)S(1)}, bf16[512,256]{1,0:T(8,128)(2,1)}, u32[]{:S(2)}) copy-start(bf16[512,256]{1,0:T(8,128)(2,1)} %constant.18.ty_ref) | copy-start | bytes 786436
  1.3 13.9 %copy-start.2 = (bf16[192,256]{1,0:T(8,128)(2,1)S(1)}, bf16[192,256]{1,0:T(8,128)(2,1)}, u32[]{:S(2)}) copy-start(bf16[192,256]{1,0:T(8,128)(2,1)} %constant.16.tx_ref) | copy-start | bytes 294916
  1.3 13.9 %copy-start.3 = (bf16[2,16,128]{2,1,0:T(8,128)(2,1)S(1)}, bf16[2,16,128]{2,1,0:T(8,128)(2,1)}, u32[]{:S(2)}) copy-start(bf16[2,16,128]{2,1,0:T(8,128)(2,1)} %constant.25.th_ref) | copy-start | bytes 24580

commit v3 on v2

--- a/solution.py
+++ b/solution.py
@@ -179,7 +179,7 @@
 def shards(velocity):
     planes, rows, cols = velocity.shape
     halo_y, halo_x = exchange(velocity)
-    tile = pick_rows(rows, 768)
+    tile = pick_rows(rows, 1536)
     per = tile // HALO
     strips = rows // HALO
     tx = weight_table(np.arange(OUT_ROWS) + HALO, np.arange(WINDOW))

time: 53 us -> 51.3 us (0.968)
  Pallas kernels: 51.1 us -> 49.7 us
    pallas_call x1, Pallas kernels: 37.3 us -> 35.8 us  [shards(): pl.pallas_call(main_kernel, grid=(planes, rows // tile), in_specs=[full,...]
where the time goes in v3:
time: 51.3 us; the launch traced here: 51 us
  Pallas kernels  49.7 us (97%)
  local copies, waits for them, and re-layouts  0.7 us (1%)
  between operations  0.67 us (1%)
    pallas_call x1, Pallas kernels, shards(): pl.pallas_call(main_kernel, grid=(planes, rows // tile), in_specs=[full,...  35.8 us
    pallas_call x1, Pallas kernels, exchange(): pl.pallas_call(exchange_kernel, in_specs=[pl.BlockSpec(memory_space=pl.AN...  13.8 us

profile of v3, /device:TPU:0, one launch (start us, length us, event | category | flops | bytes accessed | tf_op | source)
XLA Modules:
  0.0 51.0 jit_solution(14164313445580452461)
XLA Ops:
  0.6 0.0 copy-start
  0.6 0.7 %copy-done = bf16[2,16,128]{2,1,0:T(8,128)(2,1)S(1)} copy-done((bf16[2,16,128]{2,1,0:T(8,128)(2,1)S(1)}, bf16[2,16,128]{2,1,0:T(8,128)(2,1)}, u32[]{:S(2)}) %copy-start) | copy-done | bytes 8216
  1.3 0.0 copy-start.1
  1.3 0.0 copy-start.2
  1.3 0.0 copy-start.3
  1.3 13.8 %shard_map.77 = (bf16[2,3,16,3072]{3,2,1,0:T(8,128)(2,1)S(1)}, bf16[2,3,16,1536]{3,2,1,0:T(8,128)(2,1)S(1)}) custom-call(bf16[3,3072,1536]{2,1,0:T(8,128)(2,1)} %next_ref.1, bf16[2,16,128]{2,1,0:T(8,128)(2,1)S(1)} %copy-done), custom_call_target="tpu_custom_call" | custom-call | tf_op jit(solution)/shard_map/pallas_call | solution.py:113
  15.2 0.0 copy-done.1
  15.2 0.0 copy-done.2
  15.2 0.0 copy-done.3
  15.2 35.8 %shard_map.78 = (bf16[3,3072,1536]{2,1,0:T(8,128)(2,1)}, bf16[3,3072,1536]{2,1,0:T(8,128)(2,1)}) custom-call(bf16[3,3072,1536]{2,1,0:T(8,128)(2,1)} %next_ref.1, bf16[3,3072,1536]{2,1,0:T(8,128)(2,1)} %next_ref.1, bf16[3,3072,1536]{2,1,0:T(8,128)(2,1)} %next_ref.1, bf16[2,3,16,1536]{3,2,1,0:T(8,128)(2,1)S(1)} %get-tuple-element.4.before_x_ref.after_x_ref, ...), custom_call_target="tpu_custom_call" | custom-call | flops 28991029248 | bytes 84934656 | tf_op jit(solution)/shard_map/pallas_call | solution.py:202
Async XLA Ops:
  0.6 0.7 %copy-start = (bf16[2,16,128]{2,1,0:T(8,128)(2,1)S(1)}, bf16[2,16,128]{2,1,0:T(8,128)(2,1)}, u32[]{:S(2)}) copy-start(bf16[2,16,128]{2,1,0:T(8,128)(2,1)} %constant.15.table_ref) | copy-start | bytes 24580
  1.3 13.8 %copy-start.1 = (bf16[512,256]{1,0:T(8,128)(2,1)S(1)}, bf16[512,256]{1,0:T(8,128)(2,1)}, u32[]{:S(2)}) copy-start(bf16[512,256]{1,0:T(8,128)(2,1)} %constant.18.ty_ref) | copy-start | bytes 786436
  1.3 13.9 %copy-start.2 = (bf16[192,256]{1,0:T(8,128)(2,1)S(1)}, bf16[192,256]{1,0:T(8,128)(2,1)}, u32[]{:S(2)}) copy-start(bf16[192,256]{1,0:T(8,128)(2,1)} %constant.16.tx_ref) | copy-start | bytes 294916
  1.3 13.9 %copy-start.3 = (bf16[2,16,128]{2,1,0:T(8,128)(2,1)S(1)}, bf16[2,16,128]{2,1,0:T(8,128)(2,1)}, u32[]{:S(2)}) copy-start(bf16[2,16,128]{2,1,0:T(8,128)(2,1)} %constant.25.th_ref) | copy-start | bytes 24580
